TPU v7x, 32 devices: a whole 2x2x4 slice. The times are simulated.
32 devices in a mesh: grp: 2 (over x), row: 16 (over z, y, core).
Axes of the slice: x: 2, y: 2, z: 4, core: 2. Of those that a mesh axis runs over, the one named last changes fastest.
Arguments:
- matrix: bfloat16 [32, 2048, 16384], P(('grp', 'row')), parts along dimension 0, may hold values from -1 to 1
- probes: bfloat16 [16384, 128], P(('grp', 'row')), parts along dimension 0, may hold values from -6 to 6
Outputs:
- basis_out: bfloat16 [16384, 128], P(('grp', 'row')), parts along dimension 0
- sketch_out: bfloat16 [32, 4096, 128], P(('grp', 'row')), parts along dimension 0
There are 2 independent parts, one for each index of `grp`. A program takes and returns all parts, laid end to end along the dimension named above; each array names one. Nothing has to cross between parts.
All inputs are finite; a program needn't handle non-finite values.
Results may differ from a plain program's by a relative error of at most 0.012.
Values may be sent and summed in bfloat16 or wider, within the bound.
A program may use at most 192 MiB of HBM per device.

v0:
```python
import math
import jax
import jax.numpy as jnp
from jax import lax
from jax.sharding import PartitionSpec as P

GRID_ROWS = 4
ITERS = 2


def from_partner(shard, axis, bit):
    return lax.ppermute(shard, axis, [(i, i ^ 1 << bit) for i in range(lax.axis_size(axis))])


def orthonormal(product, gram_matrix, rescale):
    factor = jnp.linalg.cholesky(gram_matrix)
    solved = lax.linalg.triangular_solve(
        factor, product, left_side=False, lower=True, transpose_a=True
    )
    return (solved * rescale).astype(jnp.bfloat16)


def digit_set(device, level):
    return device // 2**level % 2 == 1


def per_device(matrix, probes):
    tile_block = matrix[0]
    tile_rows = tile_block.shape[0]
    grid_cols = lax.axis_size("row") // GRID_ROWS
    col_levels = grid_cols.bit_length() - 1
    row_levels = GRID_ROWS.bit_length() - 1
    device = lax.axis_index("row")
    rescale = math.sqrt(GRID_ROWS * tile_rows)
    current = probes
    sketch_block = None
    for iteration in range(ITERS):
        panel = current
        for level in range(col_levels):
            other = from_partner(panel, "row", level)
            panel = jnp.where(
                digit_set(device, level),
                jnp.concatenate([other, panel], 0),
                jnp.concatenate([panel, other], 0),
            )
        partial_value = lax.dot_general(
            tile_block, panel, (((0,), (0,)), ((), ())), preferred_element_type=jnp.float32
        )
        for level in range(row_levels):
            partial_value = partial_value + from_partner(
                partial_value.astype(jnp.bfloat16), "row", col_levels + level
            ).astype(partial_value.dtype)
        sketch = partial_value.astype(jnp.bfloat16)
        share_rows = sketch.shape[0] // GRID_ROWS
        grid_row = device // grid_cols
        sketch_block = lax.dynamic_slice_in_dim(sketch, grid_row * share_rows, share_rows, 0)
        image = jnp.dot(tile_block, sketch, preferred_element_type=jnp.float32)
        for level in reversed(range(col_levels)):
            half_rows = image.shape[0] // 2
            lower_part = image[:half_rows]
            upper_part = image[half_rows:]
            upward = digit_set(device, level)
            sent = jnp.where(upward, lower_part, upper_part)
            kept = jnp.where(upward, upper_part, lower_part)
            image = kept + from_partner(sent.astype(jnp.bfloat16), "row", level).astype(sent.dtype)
        local_gram = jnp.dot(
            image.T, image, precision=lax.Precision.HIGHEST, preferred_element_type=jnp.float32
        )
        gram_matrix = lax.psum(local_gram, "row")
        current = orthonormal(image, gram_matrix, rescale)
    return (current, sketch_block[None])


def solution(mesh):
    placed = (P(("grp", "row"), None, None), P(("grp", "row"), None))
    return jax.shard_map(
        per_device,
        mesh=mesh,
        in_specs=placed,
        out_specs=(P(("grp", "row"), None), P(("grp", "row"), None, None)),
        check_vma=False,
    )
```

profile of v0, /device:TPU:8, one launch (start us, length us, event | category | flops | bytes accessed | tf_op | source)
XLA Modules:
  0.0 968.9 jit_solution(17788045940890955766)
XLA Ops:
  8.3 1.3 collective-permute-done
  9.7 1.6 collective-permute-start.1
  11.3 6.8 collective-permute-done.1
  18.2 28.6 %fusion.50 = (bf16[16384,128]{0,1:T(8,128)(2,1)}, f32[16384,128]{0,1:T(8,128)}) fusion(bf16[1,2048,16384]{2,1,0:T(8,128)(2,1)} %param.5, bf16[1024,128]{0,1:T(8,128)(2,1)S(1)} %maximum_select_fusion.4, bf16[1024,128]{0,1:T(8,128)(2,1)S(1)} %collective-permute-done.1, pred[]{:T(512)S(6)} %eq.22), kind=kOutput, calls=%fused_computation.70 | convolution fusion | flops 8594391040 | bytes 80216064 | tf_op jit(solution)/shard_map/dot_general | solution.py:46
  47.0 91.8 %collective-permute-done.2 = bf16[16384,128]{0,1:T(8,128)(2,1)S(1)} collective-permute-done((bf16[16384,128]{0,1:T(8,128)(2,1)}, bf16[16384,128]{0,1:T(8,128)(2,1)S(1)}, u32[]{:S(2)}, u32[]{:S(2)}) %collective-permute-start.2) | collective-permute-done | bytes 4194336 | tf_op jit(solution)/shard_map/ppermute | solution.py:12
  138.8 5.7 fusion.14
  144.5 2.7 collective-permute-start.3
  147.1 178.2 %collective-permute-done.3 = bf16[16384,128]{0,1:T(8,128)(2,1)} collective-permute-done((bf16[16384,128]{0,1:T(8,128)(2,1)S(1)}, bf16[16384,128]{0,1:T(8,128)(2,1)}, u32[]{:S(2)}, u32[]{:S(2)}) %collective-permute-start.3) | collective-permute-done | bytes 4194336 | tf_op jit(solution)/shard_map/ppermute | solution.py:12
  325.3 33.8 %fusion.16 = f32[2048,128]{0,1:T(8,128)S(1)} fusion(bf16[1,2048,16384]{2,1,0:T(8,128)(2,1)} %param.5, bf16[16384,128]{0,1:T(8,128)(2,1)} %collective-permute-done.3, f32[16384,128]{0,1:T(8,128)} %get-tuple-element.9, bf16[16384,128]{0,1:T(8,128)(2,1)} %copy-done), kind=kOutput, calls=%fused_computation.16 | convolution fusion | flops 8600420352 | bytes 84934656 | tf_op jit(solution)/shard_map/dot_general | solution.py:57
  359.2 1.6 collective-permute-start.4
  360.8 6.7 collective-permute-done.4
  367.7 1.3 collective-permute-done.5
  369.0 1.0 fusion.46
  370.3 89.0 %all-reduce.3.cloned.1.call-done = f32[128,128]{0,1:T(8,128)} async-done(((f32[128,128]{0,1:T(8,128)}), f32[128,128]{0,1:T(8,128)}) %all-reduce.3.cloned.1.call-update) | async-done | bytes 65552 | tf_op jit(solution)/shard_map/psum | solution.py:69
  461.1 11.7 %cholesky.44 = f32[128,128]{1,0:T(8,128)S(1)} custom-call(f32[128,128]{1,0:T(8,128)S(1)} %fusion.43), custom_call_target="Cholesky" | custom-call | tf_op jit(solution)/shard_map/jit(cholesky)/cholesky | solution.py:16
  474.2 9.8 %custom-call.6 = f32[1,128,128]{1,2,0:T(8,128)S(1)} custom-call(f32[1,128,128]{2,1,0:T(8,128)S(1)} %fusion.38), custom_call_target="InvertDiagBlocksLowerTriangular" | custom-call | tf_op jit(solution)/shard_map/triangular_solve/custom-call.0 | solution.py:17
  484.5 1.3 collective-permute-done.6
  486.6 7.8 collective-permute-done.7
  494.4 28.6 %fusion.51 = (bf16[16384,128]{0,1:T(8,128)(2,1)}, f32[16384,128]{0,1:T(8,128)}) fusion(bf16[1,2048,16384]{2,1,0:T(8,128)(2,1)} %param.5, bf16[1024,128]{0,1:T(8,128)(2,1)S(1)} %maximum_select_fusion.5, bf16[1024,128]{0,1:T(8,128)(2,1)S(1)} %collective-permute-done.7, pred[]{:T(512)S(6)} %eq.22), kind=kOutput, calls=%fused_computation.71 | convolution fusion | flops 8594391040 | bytes 80216064 | tf_op jit(solution)/shard_map/dot_general | solution.py:46
  523.0 92.0 %collective-permute-done.8 = bf16[16384,128]{0,1:T(8,128)(2,1)S(1)} collective-permute-done((bf16[16384,128]{0,1:T(8,128)(2,1)}, bf16[16384,128]{0,1:T(8,128)(2,1)S(1)}, u32[]{:S(2)}, u32[]{:S(2)}) %collective-permute-start.8) | collective-permute-done | bytes 4194336 | tf_op jit(solution)/shard_map/ppermute | solution.py:12
  615.0 4.4 fusion.15
  619.4 1.5 collective-permute-start.9
  620.9 178.3 %collective-permute-done.9 = bf16[16384,128]{0,1:T(8,128)(2,1)} collective-permute-done((bf16[16384,128]{0,1:T(8,128)(2,1)S(1)}, bf16[16384,128]{0,1:T(8,128)(2,1)}, u32[]{:S(2)}, u32[]{:S(2)}) %collective-permute-start.9) | collective-permute-done | bytes 4194336 | tf_op jit(solution)/shard_map/ppermute | solution.py:12
  799.2 8.2 add_convert_fusion
  807.4 29.7 %fusion.19 = f32[2048,128]{0,1:T(8,128)S(1)} fusion(bf16[16384,128]{0,1:T(8,128)(2,1)} %add_convert_fusion, bf16[1,2048,16384]{2,1,0:T(8,128)(2,1)} %param.5), kind=kOutput, calls=%fused_computation.17 | convolution fusion | flops 8589934592 | bytes 72351744 | tf_op jit(solution)/shard_map/dot_general | solution.py:57
  837.6 7.8 collective-permute-done.10
  845.6 1.3 collective-permute-done.11
  848.0 1.3 constant_dynamic-slice_fusion
  849.3 1.3 copy.19
  850.6 85.7 %all-reduce.5.cloned.1.call-done = f32[128,128]{0,1:T(8,128)} async-done(((f32[128,128]{0,1:T(8,128)}), f32[128,128]{0,1:T(8,128)}) %all-reduce.5.cloned.1.call-update) | async-done | bytes 65552 | tf_op jit(solution)/shard_map/psum | solution.py:69
  938.0 11.7 %cholesky.55 = f32[128,128]{1,0:T(8,128)S(1)} custom-call(f32[128,128]{1,0:T(8,128)S(1)} %fusion.41), custom_call_target="Cholesky" | custom-call | tf_op jit(solution)/shard_map/jit(cholesky)/cholesky | solution.py:16
  951.1 9.8 %custom-call.7 = f32[1,128,128]{1,2,0:T(8,128)S(1)} custom-call(f32[1,128,128]{2,1,0:T(8,128)S(1)} %fusion.39), custom_call_target="InvertDiagBlocksLowerTriangular" | custom-call | tf_op jit(solution)/shard_map/triangular_solve/custom-call.0 | solution.py:17
  (37 shorter events, 12.3 us)
Async XLA Ops:
  7.2 452.2 %all-reduce.3.cloned.1.call-start = ((), (), s32[]{:S(2)}) async-start(), calls=%async_computation | async-start | bytes 131072 | tf_op jit(solution)/shard_map/psum | solution.py:69
  8.2 1.4 collective-permute-start
  9.7 8.4 collective-permute-start.1
  46.7 92.0 %collective-permute-start.2 = (bf16[16384,128]{0,1:T(8,128)(2,1)}, bf16[16384,128]{0,1:T(8,128)(2,1)S(1)}, u32[]{:S(2)}, u32[]{:S(2)}) collective-permute-start(bf16[16384,128]{0,1:T(8,128)(2,1)} %get-tuple-element.8), channel_id=1, source_target_pairs={{0,4},{1,5},{2,6},{3,7},{4,0},{5,1},{6,2},{7,3},{8,12},{9,13},{10,... | collective-permute-start | bytes 12582920 | tf_op jit(solution)/shard_map/ppermute | solution.py:12
  138.8 5.7 copy-start
  144.5 180.8 %collective-permute-start.3 = (bf16[16384,128]{0,1:T(8,128)(2,1)S(1)}, bf16[16384,128]{0,1:T(8,128)(2,1)}, u32[]{:S(2)}, u32[]{:S(2)}) collective-permute-start(bf16[16384,128]{0,1:T(8,128)(2,1)S(1)} %fusion.14), channel_id=1, source_target_pairs={{0,8},{1,9},{2,10},{3,11},{4,12},{5,13},{6,14},{7,15},{8,0},{9,1},... | collective-permute-start | bytes 12582920 | tf_op jit(solution)/shard_map/ppermute | solution.py:12
  359.2 8.3 collective-permute-start.4
  367.6 1.4 collective-permute-start.5
  370.1 566.2 %all-reduce.5.cloned.1.call-start = ((), (), s32[]{:S(2)}) async-start(), calls=%async_computation.1 | async-start | bytes 131072 | tf_op jit(solution)/shard_map/psum | solution.py:69
  484.4 1.4 collective-permute-start.6
  485.9 8.4 collective-permute-start.7
  523.0 92.0 %collective-permute-start.8 = (bf16[16384,128]{0,1:T(8,128)(2,1)}, bf16[16384,128]{0,1:T(8,128)(2,1)S(1)}, u32[]{:S(2)}, u32[]{:S(2)}) collective-permute-start(bf16[16384,128]{0,1:T(8,128)(2,1)} %get-tuple-element.10), channel_id=1, source_target_pairs={{0,4},{1,5},{2,6},{3,7},{4,0},{5,1},{6,2},{7,3},{8,12},{9,13},{10,... | collective-permute-start | bytes 12582920 | tf_op jit(solution)/shard_map/ppermute | solution.py:12
  619.4 179.8 %collective-permute-start.9 = (bf16[16384,128]{0,1:T(8,128)(2,1)S(1)}, bf16[16384,128]{0,1:T(8,128)(2,1)}, u32[]{:S(2)}, u32[]{:S(2)}) collective-permute-start(bf16[16384,128]{0,1:T(8,128)(2,1)S(1)} %fusion.15), channel_id=1, source_target_pairs={{0,8},{1,9},{2,10},{3,11},{4,12},{5,13},{6,14},{7,15},{8,0},{9,1},... | collective-permute-start | bytes 12582920 | tf_op jit(solution)/shard_map/ppermute | solution.py:12
  837.1 8.3 collective-permute-start.10
  845.5 1.4 collective-permute-start.11
Sparse Core Ops, SparseCore 0:
  370.2 89.0 all-reduce.2
  848.1 88.1 all-reduce.4
where the time goes:
time: 970 us; the launch traced here: 969 us
  waiting for transfers between devices  749 us (77%)
  matrix products  124 us (13%)
  other arithmetic  66.2 us (7%)
  between operations  14.3 us (1%)
    ppermute x12, waiting for transfers between devices, from_partner(): lax.ppermute(shard, axis, [(i, i ^ 1 << bit) for i in range(lax.axis_size...  575 us
    psum x2, waiting for transfers between devices, per_device(): gram_matrix = lax.psum(local_gram, 'row')  175 us
    dot_general x2, matrix products, per_device(): image = jnp.dot(tile_block, sketch, preferred_element_type=jnp.float32)  63.5 us
    dot_general x2, matrix products, per_device(): lax.dot_general(tile_block, panel, (((0,), (0,)), ((), ())), preferred_el...  57.2 us
    another operation x6, other arithmetic, orthonormal(): factor = jnp.linalg.cholesky(gram_matrix)  24.8 us
    another operation x4, other arithmetic, orthonormal(): lax.linalg.triangular_solve(factor, product, left_side=False, lower=True,...  20.9 us
  transfers between devices with their start and end apart: 14, of which 14 were waited for; matrix products, arithmetic and copies ran while one was open for 0% of the time, Pallas kernels for 0%

commit v1 on v0

--- a/solution.py
+++ b/solution.py
@@ -66,7 +66,7 @@
         local_gram = jnp.dot(
             image.T, image, precision=lax.Precision.HIGHEST, preferred_element_type=jnp.float32
         )
-        gram_matrix = lax.psum(local_gram, "row")
+        gram_matrix = jnp.sum(lax.all_gather(local_gram, "row"), axis=0)
         current = orthonormal(image, gram_matrix, rescale)
     return (current, sketch_block[None])
 

time: 970 us -> 873 us (0.900)
  waiting for transfers between devices: 749 us -> 647 us
    psum x2 -> x0, waiting for transfers between devices: 175 us -> none  [per_device(): gram_matrix = lax.psum(local_gram, 'row')]
    all_gather x0 -> x2, waiting for transfers between devices: none -> 74.5 us  [per_device(): gram_matrix = jnp.sum(lax.all_gather(local_gram, 'row'), axis=0)]
where the time goes in v1:
time: 873 us; the launch traced here: 869 us
  waiting for transfers between devices  647 us (74%)
  matrix products  124 us (14%)
  other arithmetic  67.1 us (8%)
  between operations  14.3 us (2%)
  starting transfers between devices  12.6 us (1%)
    ppermute x12, waiting for transfers between devices, from_partner(): lax.ppermute(shard, axis, [(i, i ^ 1 << bit) for i in range(lax.axis_size...  573 us
    all_gather x2, waiting for transfers between devices, per_device(): gram_matrix = jnp.sum(lax.all_gather(local_gram, 'row'), axis=0)  74.5 us
    dot_general x2, matrix products, per_device(): image = jnp.dot(tile_block, sketch, preferred_element_type=jnp.float32)  63.5 us
    dot_general x2, matrix products, per_device(): lax.dot_general(tile_block, panel, (((0,), (0,)), ((), ())), preferred_el...  57.2 us
    another operation x6, other arithmetic, orthonormal(): factor = jnp.linalg.cholesky(gram_matrix)  24.8 us
    another operation x4, other arithmetic, orthonormal(): lax.linalg.triangular_solve(factor, product, left_side=False, lower=True,...  20.9 us
  transfers between devices with their start and end apart: 14, of which 14 were waited for; matrix products, arithmetic and copies ran while one was open for 0% of the time, Pallas kernels for 0%

profile of v1, /device:TPU:8, one launch (start us, length us, event | category | flops | bytes accessed | tf_op | source)
XLA Modules:
  0.0 869.2 jit_solution(15765421749601292487)
XLA Ops:
  8.3 1.3 collective-permute-done
  9.7 1.6 collective-permute-start.1
  11.3 6.8 collective-permute-done.1
  18.2 28.6 %fusion.50 = (bf16[16384,128]{0,1:T(8,128)(2,1)}, f32[16384,128]{0,1:T(8,128)}) fusion(bf16[1,2048,16384]{2,1,0:T(8,128)(2,1)} %param.5, bf16[1024,128]{0,1:T(8,128)(2,1)S(1)} %maximum_select_fusion.4, bf16[1024,128]{0,1:T(8,128)(2,1)S(1)} %collective-permute-done.1, pred[]{:T(512)S(6)} %eq.22), kind=kOutput, calls=%fused_computation.70 | convolution fusion | flops 8594391040 | bytes 80216064 | tf_op jit(solution)/shard_map/dot_general | solution.py:46
  47.0 91.8 %collective-permute-done.2 = bf16[16384,128]{0,1:T(8,128)(2,1)S(1)} collective-permute-done((bf16[16384,128]{0,1:T(8,128)(2,1)}, bf16[16384,128]{0,1:T(8,128)(2,1)S(1)}, u32[]{:S(2)}, u32[]{:S(2)}) %collective-permute-start.2) | collective-permute-done | bytes 4194336 | tf_op jit(solution)/shard_map/ppermute | solution.py:12
  138.8 5.7 fusion.14
  144.5 2.7 collective-permute-start.3
  147.1 178.2 %collective-permute-done.3 = bf16[16384,128]{0,1:T(8,128)(2,1)} collective-permute-done((bf16[16384,128]{0,1:T(8,128)(2,1)S(1)}, bf16[16384,128]{0,1:T(8,128)(2,1)}, u32[]{:S(2)}, u32[]{:S(2)}) %collective-permute-start.3) | collective-permute-done | bytes 4194336 | tf_op jit(solution)/shard_map/ppermute | solution.py:12
  325.3 33.8 %fusion.16 = f32[2048,128]{0,1:T(8,128)S(1)} fusion(bf16[1,2048,16384]{2,1,0:T(8,128)(2,1)} %param.5, bf16[16384,128]{0,1:T(8,128)(2,1)} %collective-permute-done.3, f32[16384,128]{0,1:T(8,128)} %get-tuple-element.11, bf16[16384,128]{0,1:T(8,128)(2,1)} %copy-done), kind=kOutput, calls=%fused_computation.16 | convolution fusion | flops 8600420352 | bytes 84934656 | tf_op jit(solution)/shard_map/dot_general | solution.py:57
  359.2 1.6 collective-permute-start.4
  360.8 6.7 collective-permute-done.4
  367.7 1.3 collective-permute-done.5
  370.3 39.0 %all-gather.5.cloned.1.call-done = f32[2048,128]{1,0:T(8,128)} async-done(((f32[128,128]{1,0:T(8,128)}), f32[2048,128]{1,0:T(8,128)}) %all-gather.5.cloned.1.call-update) | async-done | bytes 1048592 | tf_op jit(solution)/shard_map/all_gather | solution.py:69
  409.3 1.3 reduce_sum.18
  410.7 11.7 %cholesky.44 = f32[128,128]{1,0:T(8,128)S(1)} custom-call(f32[128,128]{1,0:T(8,128)S(1)} %fusion.43), custom_call_target="Cholesky" | custom-call | tf_op jit(solution)/shard_map/jit(cholesky)/cholesky | solution.py:16
  423.7 9.8 %custom-call.6 = f32[1,128,128]{1,2,0:T(8,128)S(1)} custom-call(f32[1,128,128]{2,1,0:T(8,128)S(1)} %fusion.38), custom_call_target="InvertDiagBlocksLowerTriangular" | custom-call | tf_op jit(solution)/shard_map/triangular_solve/custom-call.0 | solution.py:17
  436.8 7.3 collective-permute-done.7
  444.0 28.6 %fusion.51 = (bf16[16384,128]{0,1:T(8,128)(2,1)}, f32[16384,128]{0,1:T(8,128)}) fusion(bf16[1,2048,16384]{2,1,0:T(8,128)(2,1)} %param.5, bf16[1024,128]{0,1:T(8,128)(2,1)S(1)} %maximum_select_fusion.5, bf16[1024,128]{0,1:T(8,128)(2,1)S(1)} %collective-permute-done.7, pred[]{:T(512)S(6)} %eq.22), kind=kOutput, calls=%fused_computation.71 | convolution fusion | flops 8594391040 | bytes 80216064 | tf_op jit(solution)/shard_map/dot_general | solution.py:46
  472.6 1.5 collective-permute-start.8
  474.1 90.6 %collective-permute-done.8 = bf16[16384,128]{0,1:T(8,128)(2,1)S(1)} collective-permute-done((bf16[16384,128]{0,1:T(8,128)(2,1)}, bf16[16384,128]{0,1:T(8,128)(2,1)S(1)}, u32[]{:S(2)}, u32[]{:S(2)}) %collective-permute-start.8) | collective-permute-done | bytes 4194336 | tf_op jit(solution)/shard_map/ppermute | solution.py:12
  564.8 4.4 fusion.15
  569.2 2.3 collective-permute-start.9
  571.5 178.4 %collective-permute-done.9 = bf16[16384,128]{0,1:T(8,128)(2,1)} collective-permute-done((bf16[16384,128]{0,1:T(8,128)(2,1)S(1)}, bf16[16384,128]{0,1:T(8,128)(2,1)}, u32[]{:S(2)}, u32[]{:S(2)}) %collective-permute-start.9) | collective-permute-done | bytes 4194336 | tf_op jit(solution)/shard_map/ppermute | solution.py:12
  749.9 8.2 add_convert_fusion
  758.1 29.7 %fusion.19 = f32[2048,128]{0,1:T(8,128)S(1)} fusion(bf16[16384,128]{0,1:T(8,128)(2,1)} %add_convert_fusion, bf16[1,2048,16384]{2,1,0:T(8,128)(2,1)} %param.5), kind=kOutput, calls=%fused_computation.17 | convolution fusion | flops 8589934592 | bytes 72351744 | tf_op jit(solution)/shard_map/dot_general | solution.py:57
  788.5 7.6 collective-permute-done.10
  796.3 1.3 collective-permute-done.11
  798.7 1.3 constant_dynamic-slice_fusion
  800.0 1.3 copy.22
  801.4 35.6 %all-gather.7.cloned.1.call-done = f32[2048,128]{1,0:T(8,128)} async-done(((f32[128,128]{1,0:T(8,128)}), f32[2048,128]{1,0:T(8,128)}) %all-gather.7.cloned.1.call-update) | async-done | bytes 1048592 | tf_op jit(solution)/shard_map/all_gather | solution.py:69
  838.3 11.7 %cholesky.55 = f32[128,128]{1,0:T(8,128)S(1)} custom-call(f32[128,128]{1,0:T(8,128)S(1)} %fusion.41), custom_call_target="Cholesky" | custom-call | tf_op jit(solution)/shard_map/jit(cholesky)/cholesky | solution.py:16
  851.4 9.8 %custom-call.7 = f32[1,128,128]{1,2,0:T(8,128)S(1)} custom-call(f32[1,128,128]{2,1,0:T(8,128)S(1)} %fusion.39), custom_call_target="InvertDiagBlocksLowerTriangular" | custom-call | tf_op jit(solution)/shard_map/triangular_solve/custom-call.0 | solution.py:17
  (39 shorter events, 13.3 us)
Async XLA Ops:
  7.2 402.1 %all-gather.5.cloned.1.call-start = ((), (), s32[]{:S(2)}) async-start(), calls=%async_computation | async-start | bytes 1114112 | tf_op jit(solution)/shard_map/all_gather | solution.py:69
  8.2 1.4 collective-permute-start
  9.7 8.4 collective-permute-start.1
  46.7 92.0 %collective-permute-start.2 = (bf16[16384,128]{0,1:T(8,128)(2,1)}, bf16[16384,128]{0,1:T(8,128)(2,1)S(1)}, u32[]{:S(2)}, u32[]{:S(2)}) collective-permute-start(bf16[16384,128]{0,1:T(8,128)(2,1)} %get-tuple-element.10), channel_id=1, source_target_pairs={{0,4},{1,5},{2,6},{3,7},{4,0},{5,1},{6,2},{7,3},{8,12},{9,13},{10,... | collective-permute-start | bytes 12582920 | tf_op jit(solution)/shard_map/ppermute | solution.py:12
  138.8 5.7 copy-start
  144.5 180.8 %collective-permute-start.3 = (bf16[16384,128]{0,1:T(8,128)(2,1)S(1)}, bf16[16384,128]{0,1:T(8,128)(2,1)}, u32[]{:S(2)}, u32[]{:S(2)}) collective-permute-start(bf16[16384,128]{0,1:T(8,128)(2,1)S(1)} %fusion.14), channel_id=1, source_target_pairs={{0,8},{1,9},{2,10},{3,11},{4,12},{5,13},{6,14},{7,15},{8,0},{9,1},... | collective-permute-start | bytes 12582920 | tf_op jit(solution)/shard_map/ppermute | solution.py:12
  359.2 8.3 collective-permute-start.4
  367.6 1.4 collective-permute-start.5
  370.1 466.8 %all-gather.7.cloned.1.call-start = ((), (), s32[]{:S(2)}) async-start(), calls=%async_computation.1 | async-start | bytes 1114112 | tf_op jit(solution)/shard_map/all_gather | solution.py:69
  434.0 1.4 collective-permute-start.6
  435.5 8.5 collective-permute-start.7
  472.6 92.1 %collective-permute-start.8 = (bf16[16384,128]{0,1:T(8,128)(2,1)}, bf16[16384,128]{0,1:T(8,128)(2,1)S(1)}, u32[]{:S(2)}, u32[]{:S(2)}) collective-permute-start(bf16[16384,128]{0,1:T(8,128)(2,1)} %get-tuple-element.12), channel_id=1, source_target_pairs={{0,4},{1,5},{2,6},{3,7},{4,0},{5,1},{6,2},{7,3},{8,12},{9,13},{10,... | collective-permute-start | bytes 12582920 | tf_op jit(solution)/shard_map/ppermute | solution.py:12
  569.2 180.7 %collective-permute-start.9 = (bf16[16384,128]{0,1:T(8,128)(2,1)S(1)}, bf16[16384,128]{0,1:T(8,128)(2,1)}, u32[]{:S(2)}, u32[]{:S(2)}) collective-permute-start(bf16[16384,128]{0,1:T(8,128)(2,1)S(1)} %fusion.15), channel_id=1, source_target_pairs={{0,8},{1,9},{2,10},{3,11},{4,12},{5,13},{6,14},{7,15},{8,0},{9,1},... | collective-permute-start | bytes 12582920 | tf_op jit(solution)/shard_map/ppermute | solution.py:12
  787.9 8.3 collective-permute-start.10
  796.3 1.4 collective-permute-start.11
Sparse Core Ops, SparseCore 0:
  370.2 39.0 all-gather.4
  798.8 38.0 all-gather.6
